TPU v7x, 32 devices: a whole 2x2x4 slice. The times are simulated.
32 devices in a mesh: groups: 2 (over y), chan: 4 (over z), win: 2 (over x), sub: 2 (over core).
Axes of the slice: x: 2, y: 2, z: 4, core: 2. Of those that a mesh axis runs over, the one named last changes fastest.
Arguments:
- records: bfloat16 [2048, 1792], P(('groups', 'chan', 'sub'), 'win'), parts along dimension 0, may hold values from -6 to 6
- lag_weights: float32 [65], replicated, may hold values from -4 to 4
- probes: bfloat16 [2048, 64], P(('groups', 'chan', 'sub')), parts along dimension 0, may hold values from -6 to 6
Outputs:
- covariance: bfloat16 [3, 2048, 256], P(None, ('groups', 'chan', 'sub'), 'win'), parts along dimension 1
- subspace: float32 [2048, 64], P(('groups', 'chan', 'sub')), parts along dimension 0
There are 2 independent parts, one for each index of `groups`. A program takes and returns all parts, laid end to end along the dimension named above; an argument that names none is the same for every part. Nothing has to cross between parts.
All inputs are finite; a program needn't handle non-finite values.
Results may differ from a plain program's by a relative error of at most 0.0051.
Values may be sent and summed in bfloat16 or wider, within the bound.
A program may use at most 64 MiB of HBM per device.

v0:
```python
import jax
import jax.numpy as jnp
from jax import lax
from jax.sharding import PartitionSpec as P

CB = 256
MAXLAG = 32


def extended(block, sides, width):
    for axis, dim in sides:
        count = lax.axis_size(axis)
        forward = [(i, i + 1) for i in range(count - 1)]
        backward = [(target, source) for source, target in forward]
        low = lax.ppermute(
            lax.slice_in_dim(block, block.shape[dim] - width, None, axis=dim), axis, forward
        )
        high = lax.ppermute(lax.slice_in_dim(block, 0, width, axis=dim), axis, backward)
        block = jnp.concatenate([low, block, high], axis=dim)
    return block


def filter_lags(padded, weights, width):

    def add_lag(lag_index, running):
        window = lax.dynamic_slice_in_dim(padded, lag_index, width, 1).astype(jnp.float32)
        return running + weights[lag_index] * window

    return lax.fori_loop(
        0, weights.shape[0], add_lag, jnp.zeros((padded.shape[0], width), jnp.float32)
    )


def body(records, lag_weights, probes):
    row_count = records.shape[0]
    width = records.shape[1]
    chan_count = lax.axis_size("chan")
    half_cycle = chan_count // 2
    samples = width * lax.axis_size("win")
    my_index = lax.axis_index("chan")
    symmetric = 0.5 * (lag_weights + lag_weights[::-1])
    padded = extended(records, (("win", 1),), MAXLAG)
    filtered = filter_lags(padded, symmetric, width).astype(jnp.bfloat16)
    contract = (((1,), (1,)), ((), ()))
    partial_value = lax.dot_general(
        records,
        lax.all_gather(filtered, ("chan", "sub"), axis=0, tiled=True),
        contract,
        preferred_element_type=jnp.float32,
    )
    blocks = partial_value.reshape(row_count, chan_count, CB)
    chosen = (my_index + jnp.arange(half_cycle + 1)) % chan_count
    stacked = jnp.take(blocks, chosen, axis=1).transpose(1, 0, 2)
    local_products = lax.dot_general(
        filtered, probes, (((0,), (0,)), ((), ())), preferred_element_type=jnp.float32
    )
    window_products = lax.psum(local_products, ("chan", "sub"))
    images = jnp.dot(records.astype(jnp.float32), window_products, precision=lax.Precision.HIGHEST)
    summed = lax.psum_scatter(stacked, "win", scatter_dimension=2, tiled=True)
    covariance = (summed / samples).astype(jnp.bfloat16)
    images = lax.psum(images, "win") / samples
    local_gram = lax.dot_general(
        images, images, (((0,), (0,)), ((), ())), precision=lax.Precision.HIGHEST
    )
    gram_matrix = lax.psum(local_gram, ("chan", "sub")) / (CB * chan_count)
    factor = jnp.linalg.cholesky(gram_matrix)
    subspace = lax.linalg.triangular_solve(
        factor, images, left_side=False, lower=True, transpose_a=True
    )
    return (covariance, subspace)


def solution(mesh):
    return jax.shard_map(
        body,
        mesh=mesh,
        in_specs=(P(("groups", "chan", "sub"), "win"), P(), P(("groups", "chan", "sub"), None)),
        out_specs=(P(None, ("groups", "chan", "sub"), "win"), P(("groups", "chan", "sub"), None)),
        check_vma=False,
    )
```

profile of v0, /device:TPU:1, one launch (start us, length us, event | category | flops | bytes accessed | tf_op | source)
XLA Modules:
  0.0 228.5 jit_solution(633942177523527644)
XLA Ops:
  7.2 0.9 fusion.14
  8.1 3.9 %collective-permute-start = (bf16[128,32]{1,0:T(8,128)(2,1)S(1)}, bf16[128,32]{1,0:T(8,128)(2,1)S(1)}, u32[]{:S(2)}, u32[]{:S(2)}) collective-permute-start(bf16[128,32]{1,0:T(8,128)(2,1)S(1)} %get-tuple-element.105), channel_id=1, source_target_pairs={{0,2},{1,3},{4,6},{5,7},{8,10},{9,11},{12,14},{13,15},{16,18},{17,... | collective-permute-start | bytes 24584 | tf_op jit(solution)/shard_map/ppermute | solution.py:15
  12.0 1.3 collective-permute-start.1
  14.7 1.9 collective-permute-done.1
  16.7 1.1 pad_maximum_fusion
  17.8 92.8 %while.14 = (s32[]{:T(128)}, f32[128,896]{1,0:T(8,128)S(1)}, f32[65]{0:T(128)S(1)}, bf16[128,960]{1,0:T(8,128)(2,1)S(1)}, s32[]{:T(128)}, /*index=5*/s32[]{:T(128)}) while((s32[]{:T(128)}, f32[128,896]{1,0:T(8,128)S(1)}, f32[65]{0:T(128)S(1)}, bf16[128,960]{1,0:T(8,128)(2,1)S(1)}, s32[]{:T(128)}, /*index=5*/s32[]{:T(128)}) %tuple.37), condition=%wide.region_1.0_spmd.clone, body=%wide.region_0.0_spmd.clone.sunk | while | flops 458755 | bytes 1146979 | solution.py:29
  18.4 0.8 select_add_fusion.2
  19.8 0.8 select_add_fusion.2
  21.2 0.8 select_add_fusion.2
  22.7 0.8 select_add_fusion.2
  24.1 0.8 select_add_fusion.2
  25.5 0.8 select_add_fusion.2
  26.9 0.8 select_add_fusion.2
  28.4 0.8 select_add_fusion.2
  29.8 0.8 select_add_fusion.2
  31.2 0.8 select_add_fusion.2
  32.7 0.8 select_add_fusion.2
  34.1 0.8 select_add_fusion.2
  35.5 0.8 select_add_fusion.2
  36.9 0.8 select_add_fusion.2
  38.4 0.8 select_add_fusion.2
  39.8 0.8 select_add_fusion.2
  41.2 0.8 select_add_fusion.2
  42.7 0.8 select_add_fusion.2
  44.1 0.8 select_add_fusion.2
  45.5 0.8 select_add_fusion.2
  46.9 0.8 select_add_fusion.2
  48.4 0.8 select_add_fusion.2
  49.8 0.8 select_add_fusion.2
  51.2 0.8 select_add_fusion.2
  52.6 0.8 select_add_fusion.2
  54.1 0.8 select_add_fusion.2
  55.5 0.8 select_add_fusion.2
  56.9 0.8 select_add_fusion.2
  79.8 0.8 select_add_fusion.2
  106.9 0.8 select_add_fusion.2
  110.7 1.0 fusion.16
  112.6 55.2 %all-reduce.2.cloned.1.call-done = f32[896,64]{1,0:T(8,128)} async-done(((f32[896,64]{1,0:T(8,128)}), f32[896,64]{1,0:T(8,128)}) %all-reduce.2.cloned.1.call-update) | async-done | bytes 229392 | tf_op jit(solution)/shard_map/psum | solution.py:57
  167.8 1.6 convolution_bitcast_fusion
  169.3 6.3 %psum.22 = f32[128,64]{0,1:T(8,128)S(1)} all-reduce(f32[128,64]{0,1:T(8,128)S(1)} %convolution_bitcast_fusion), channel_id=1, replica_groups=mesh['groups'=2,'chan'=4,'win'=2,'sub'=2] {'win'}, use_global_device_ids=true, to_apply=%region_4.5 | all-reduce | flops 8192 | bytes 65536 | tf_op jit(solution)/shard_map/psum | solution.py:61
  175.8 26.7 %psum.23 = f32[64,64]{0,1:T(8,128)S(1)} all-reduce(f32[64,64]{0,1:T(8,128)S(1)} %fusion.5), channel_id=1, replica_groups=mesh['groups'=2,'chan'=4,'win'=2,'sub'=2] {'chan','sub'}, use_global_device_ids=true, to_apply=%region_5.6 | all-reduce | flops 4096 | bytes 32768 | tf_op jit(solution)/shard_map/psum | solution.py:65
  202.6 2.1 fusion.15
  205.5 0.8 broadcast_select_fusion
  206.4 5.8 %cholesky.16 = f32[64,64]{1,0:T(8,128)S(1)} custom-call(f32[64,64]{1,0:T(8,128)S(1)} %fusion.3), custom_call_target="Cholesky" | custom-call | tf_op jit(solution)/shard_map/jit(cholesky)/cholesky | solution.py:66
  213.6 4.9 %custom-call.6 = f32[1,64,64]{1,2,0:T(8,128)S(1)} custom-call(f32[1,64,64]{2,1,0:T(8,128)S(1)} %fusion), custom_call_target="InvertDiagBlocksLowerTriangular" | custom-call | tf_op jit(solution)/shard_map/triangular_solve | solution.py:67
  218.5 0.9 fusion.1
  219.4 1.0 reduce-scatter.2.cloned.1.call-done
  220.4 1.6 multiply_convert_fusion
  (130 shorter events, 71.5 us)
Async XLA Ops:
  7.2 103.5 %copy-start = (bf16[128,64]{0,1:T(8,128)(2,1)S(1)}, bf16[128,64]{0,1:T(8,128)(2,1)}, u32[]{:S(2)}) copy-start(bf16[128,64]{0,1:T(8,128)(2,1)} %param.7) | copy-start | bytes 49156
  7.2 160.6 %all-reduce.2.cloned.1.call-start = ((), (), s32[]{:S(2)}) async-start(), calls=%async_computation.3 | async-start | bytes 917504 | tf_op jit(solution)/shard_map/psum | solution.py:57
  8.1 6.7 %collective-permute-start = (bf16[128,32]{1,0:T(8,128)(2,1)S(1)}, bf16[128,32]{1,0:T(8,128)(2,1)S(1)}, u32[]{:S(2)}, u32[]{:S(2)}) collective-permute-start(bf16[128,32]{1,0:T(8,128)(2,1)S(1)} %get-tuple-element.105), channel_id=1, source_target_pairs={{0,2},{1,3},{4,6},{5,7},{8,10},{9,11},{12,14},{13,15},{16,18},{17,... | collective-permute-start | bytes 24584 | tf_op jit(solution)/shard_map/ppermute | solution.py:15
  12.0 4.7 %collective-permute-start.1 = (bf16[128,32]{1,0:T(8,128)(2,1)S(1)}, bf16[128,32]{1,0:T(8,128)(2,1)S(1)}, u32[]{:S(2)}, u32[]{:S(2)}) collective-permute-start(bf16[128,32]{1,0:T(8,128)(2,1)S(1)} %get-tuple-element.106), channel_id=1, source_target_pairs={{2,0},{3,1},{6,4},{7,5},{10,8},{11,9},{14,12},{15,13},{18,16},{19,... | collective-permute-start | bytes 24584 | tf_op jit(solution)/shard_map/ppermute | solution.py:18
  110.6 57.2 %copy-start.1 = (bf16[128,896]{1,0:T(8,128)(2,1)S(1)}, bf16[128,896]{1,0:T(8,128)(2,1)}, u32[]{:S(2)}) copy-start(bf16[128,896]{1,0:T(8,128)(2,1)} %param.5) | copy-start | bytes 688132
  110.6 1.1 copy-start.2
  111.7 90.9 %all-gather.2.cloned.1.call-start = ((), (), s32[]{:S(2)}) async-start(), calls=%async_computation.1 | async-start | bytes 2064384 | tf_op jit(solution)/shard_map/all_gather | solution.py:47
  112.5 108.0 %reduce-scatter.2.cloned.1.call-start = ((), (), s32[]{:S(2)}) async-start(), calls=%async_computation.2 | async-start | bytes 589824 | tf_op jit(solution)/shard_map/reduce_scatter | solution.py:59
Sparse Core Ops, SparseCore 0:
  111.8 55.8 all-reduce.1
  169.5 28.4 all-gather.1
  206.5 13.8 reduce-scatter.1
where the time goes:
time: 233 us; the launch traced here: 229 us
  other arithmetic  69.5 us (30%)
  waiting for transfers between devices  58.9 us (25%)
  local copies, waits for them, and re-layouts  40.6 us (17%)
  blocking collectives  33 us (14%)
  between operations  13.9 us (6%)
  matrix products  5.77 us (2%)
  starting transfers between devices  5.35 us (2%)
    psum x1, waiting for transfers between devices, body(): window_products = lax.psum(local_products, ('chan', 'sub'))  55.2 us
    add x65, other arithmetic, add_lag(): return running + weights[lag_index] * window  53.2 us
    dynamic_slice x65, local copies, waits for them, and re-layouts, add_lag(): return running + weights[lag_index] * window  38.1 us
    psum x1, blocking collectives, body(): gram_matrix = lax.psum(local_gram, ('chan', 'sub')) / (CB * chan_count)  26.7 us
    another operation x3, other arithmetic, body(): factor = jnp.linalg.cholesky(gram_matrix)  6.52 us
    psum x1, blocking collectives, body(): images = lax.psum(images, 'win') / samples  6.3 us
    another operation x2, other arithmetic, body(): lax.linalg.triangular_solve(factor, images, left_side=False, lower=True,...  5.56 us
  transfers between devices with their start and end apart: 5, of which 3 were waited for; matrix products, arithmetic and copies ran while one was open for 7% of the time, Pallas kernels for 0%

commit v1 on v0

v1 whole, which is shorter than its diff:
```python
import functools

import jax
import jax.numpy as jnp
from jax import lax
from jax.experimental import pallas as pl
from jax.experimental.pallas import tpu as pltpu
from jax.sharding import PartitionSpec as P

MESH = pl.DeviceIdType.MESH
MAXLAG = 32
LANES = 128
HIGHEST = lax.Precision.HIGHEST


def dot_rows(a, b, precision=None):
    return lax.dot_general(
        a, b, (((1,), (1,)), ((), ())), precision=precision, preferred_element_type=jnp.float32
    )


def halves(x):
    high = x.astype(jnp.bfloat16)
    return high, (x - high.astype(jnp.float32)).astype(jnp.bfloat16)


def banded(weights):
    count = weights.shape[1]
    start = LANES - MAXLAG
    lag = lax.broadcasted_iota(jnp.int32, (count, 3 * LANES), 0)
    place = lax.broadcasted_iota(jnp.int32, (count, 3 * LANES), 1)
    forward = jnp.where(place == lag + start, 0.5, 0.0)
    backward = jnp.where(place == start + count - 1 - lag, 0.5, 0.0)
    row = jnp.dot(weights, forward + backward, precision=HIGHEST)
    row = jnp.broadcast_to(row, (LANES, 3 * LANES))
    return pltpu.roll(row, 0, 1, stride=1, stride_axis=0)


def inverse_factor(gram):
    k = gram.shape[0]
    rows = lax.broadcasted_iota(jnp.int32, (k, k), 0)
    columns = lax.broadcasted_iota(jnp.int32, (k, k), 1)
    eye = jnp.where(rows == columns, 1.0, 0.0)
    m = jnp.concatenate([gram, eye], axis=1)
    below = lax.broadcasted_iota(jnp.int32, (k, 1), 0)
    for i in range(k - 1):
        column = m[:, i : i + 1]
        factor = jnp.where(below > i, column / m[i : i + 1, i : i + 1], 0.0)
        m = m - factor * m[i : i + 1, :]
    pivots = jnp.sum(m[:, :k] * eye, axis=1, keepdims=True)
    return m[:, k:] / jnp.sqrt(pivots)


def kernel(
    chans, wins, samples,
    r_ref, w_ref, p_ref,
    cov_ref, sub_ref,
    g, pg, ext, filt, part, sendp, recvp, im, ib, gb,
    local_sem, r_send, r_recv, p_send, p_recv, h_send, h_recv,
    c_send, c_recv, i_send, i_recv, g_send, g_recv,
):
    z = lax.axis_index("chan")
    s = lax.axis_index("sub")
    w = lax.axis_index("win")
    rows, width = r_ref.shape
    dist = cov_ref.shape[0]
    part_width = cov_ref.shape[2]
    peers = 2 * chans
    me = z * 2 + s
    other = 1 - s

    barrier = pltpu.get_barrier_semaphore()

    def greet(o, carry):
        t = lax.rem(me + o, peers)
        pl.semaphore_signal(
            barrier, inc=1, device_id={"chan": t // 2, "sub": t % 2}, device_id_type=MESH
        )
        return carry

    lax.fori_loop(1, peers, greet, 0)
    for o in range(1, wins):
        pl.semaphore_signal(
            barrier, inc=1, device_id={"win": lax.rem(w + o, wins)}, device_id_type=MESH
        )
    pl.semaphore_wait(barrier, peers - 1 + wins - 1)

    def rows_of(sub):
        return pl.ds(pl.multiple_of(sub * rows, rows), rows)

    def to(way):
        if way == 2:
            return {"sub": other}
        return {"chan": z + (1 if way == 1 else -1)}

    def copies(j, way, source_r=None, source_p=None):
        place = rows_of(s)
        return [
            pltpu.make_async_remote_copy(
                src_ref=p_ref if source_p is not None else pg.at[j, place],
                dst_ref=pg.at[j, place],
                send_sem=p_send.at[j, way],
                recv_sem=p_recv.at[j, s],
                device_id=to(way),
                device_id_type=MESH,
            ),
            pltpu.make_async_remote_copy(
                src_ref=r_ref if source_r is not None else g.at[j, place],
                dst_ref=g.at[j, place],
                send_sem=r_send.at[j, way],
                recv_sem=r_recv.at[j, s],
                device_id=to(way),
                device_id_type=MESH,
            ),
        ]

    def landed(j, sub):
        place = rows_of(sub)
        for buffer, sends, receives in ((pg, p_send, p_recv), (g, r_send, r_recv)):
            pltpu.make_async_remote_copy(
                src_ref=buffer.at[j, place],
                dst_ref=buffer.at[j, place],
                send_sem=sends.at[j, 2],
                recv_sem=receives.at[j, sub],
                device_id={"sub": other},
                device_id_type=MESH,
            ).wait_recv()

    def halo(up):
        source = pl.ds(width - LANES, LANES) if up else pl.ds(0, LANES)
        target = pl.ds(0, LANES) if up else pl.ds(width + LANES, LANES)
        return pltpu.make_async_remote_copy(
            src_ref=r_ref.at[:, source],
            dst_ref=ext.at[:, target],
            send_sem=h_send.at[int(up)],
            recv_sem=h_recv.at[int(up)],
            device_id={"win": w + (1 if up else -1)},
            device_id_type=MESH,
        )

    def start_all(items):
        for item in items:
            item.start()

    @pl.when(w < wins - 1)
    def _():
        halo(True).start()

    @pl.when(w > 0)
    def _():
        halo(False).start()

    @pl.when(z < chans - 1)
    def _():
        start_all(copies(z, 1, True, True))

    @pl.when(z > 0)
    def _():
        start_all(copies(z, 0, True, True))

    start_all(copies(z, 2, True, True))
    local = [
        pltpu.make_async_copy(p_ref, pg.at[z, rows_of(s)], local_sem.at[0]),
        pltpu.make_async_copy(r_ref, g.at[z, rows_of(s)], local_sem.at[1]),
    ]
    start_all(local)

    @pl.when(w == 0)
    def _():
        ext[:, :LANES] = jnp.zeros((rows, LANES), ext.dtype)

    @pl.when(w == wins - 1)
    def _():
        ext[:, LANES + width :] = jnp.zeros((rows, LANES), ext.dtype)

    ext[:, LANES : LANES + width] = r_ref[...]
    im[...] = jnp.zeros_like(im)
    band_high, band_low = halves(banded(w_ref[...]))

    @pl.when(w > 0)
    def _():
        halo(True).wait_recv()

    @pl.when(w < wins - 1)
    def _():
        halo(False).wait_recv()

    for b in range(width // LANES):
        window = ext[:, b * LANES : (b + 3) * LANES]
        value = dot_rows(window, band_high) + dot_rows(window, band_low)
        filt[:, b * LANES : (b + 1) * LANES] = value.astype(filt.dtype)

    def part_copy(d, o):
        t = lax.rem(w + o, wins)
        return pltpu.make_async_remote_copy(
            src_ref=sendp.at[d, t],
            dst_ref=recvp.at[d, w],
            send_sem=c_send.at[d, t],
            recv_sem=c_recv.at[d, w],
            device_id={"win": t},
            device_id_type=MESH,
        )

    def block(j):
        value = dot_rows(filt[...], g[j])
        d = lax.rem(j - z + chans, chans)
        high, low = halves(value)
        probes = pg[j]
        im[...] += jnp.dot(high, probes, preferred_element_type=jnp.float32) + jnp.dot(
            low, probes, preferred_element_type=jnp.float32
        )

        @pl.when(d < dist)
        def _():
            for t in range(wins):
                piece = value[:, t * part_width : (t + 1) * part_width]
                part[d, t] = piece
                sendp[d, t] = piece.astype(sendp.dtype)
            for o in range(1, wins):
                part_copy(d, o).start()

    for item in local:
        item.wait()
    landed(z, other)
    block(z)

    def hop(h, carry):
        above, below = z + h, z - h

        @pl.when(above < chans)
        def _():
            landed(above, s)

            @pl.when(z > 0)
            def _():
                start_all(copies(above, 0))

            start_all(copies(above, 2))

        @pl.when(below >= 0)
        def _():
            landed(below, s)

            @pl.when(z < chans - 1)
            def _():
                start_all(copies(below, 1))

            start_all(copies(below, 2))

        @pl.when(above < chans)
        def _():
            landed(above, other)
            block(above)

        @pl.when(below >= 0)
        def _():
            landed(below, other)
            block(below)

        return carry

    lax.fori_loop(1, chans, hop, 0)

    ib[w] = im[...]

    def image_copy(o):
        t = lax.rem(w + o, wins)
        return pltpu.make_async_remote_copy(
            src_ref=ib.at[w],
            dst_ref=ib.at[w],
            send_sem=i_send.at[t],
            recv_sem=i_recv.at[w],
            device_id={"win": t},
            device_id_type=MESH,
        )

    def image_landed(o):
        t = lax.rem(w + o, wins)
        return pltpu.make_async_remote_copy(
            src_ref=ib.at[t],
            dst_ref=ib.at[t],
            send_sem=i_send.at[t],
            recv_sem=i_recv.at[t],
            device_id={"win": t},
            device_id_type=MESH,
        )

    for o in range(1, wins):
        image_copy(o).start()
    for o in range(1, wins):
        image_landed(o).wait_recv()
    images = ib[0]
    for t in range(1, wins):
        images = images + ib[t]
    images = images * (1.0 / samples)
    gb[me] = lax.dot_general(
        images, images, (((0,), (0,)), ((), ())), precision=HIGHEST,
        preferred_element_type=jnp.float32,
    )

    def gram_copy(o, slot):
        t = lax.rem(me + o, peers)
        at = t if slot else me
        return pltpu.make_async_remote_copy(
            src_ref=gb.at[at],
            dst_ref=gb.at[at],
            send_sem=g_send.at[t],
            recv_sem=g_recv.at[at],
            device_id={"chan": t // 2, "sub": t % 2},
            device_id_type=MESH,
        )

    def gram_start(o, carry):
        gram_copy(o, False).start()
        return carry

    lax.fori_loop(1, peers, gram_start, 0)

    def finish(d, carry):
        total = part[d, w]
        for o in range(1, wins):
            t = lax.rem(w + o, wins)
            pltpu.make_async_remote_copy(
                src_ref=recvp.at[d, t],
                dst_ref=recvp.at[d, t],
                send_sem=c_send.at[d, t],
                recv_sem=c_recv.at[d, t],
                device_id={"win": t},
                device_id_type=MESH,
            ).wait_recv()
            total = total + recvp[d, t].astype(jnp.float32)
        cov_ref[d] = (total * (1.0 / samples)).astype(cov_ref.dtype)
        return carry

    lax.fori_loop(0, dist, finish, 0)

    def gram_landed(o, carry):
        gram_copy(o, True).wait_recv()
        return carry

    lax.fori_loop(1, peers, gram_landed, 0)
    gram = lax.fori_loop(1, peers, lambda t, total: total + gb[t], gb[0])
    inverse = inverse_factor(gram * (1.0 / (rows * peers)))
    sub_ref[...] = dot_rows(images, inverse, HIGHEST)

    @pl.when(w < wins - 1)
    def _():
        halo(True).wait_send()

    @pl.when(w > 0)
    def _():
        halo(False).wait_send()

    def drain(j, carry):
        @pl.when((j >= z) & (z > 0))
        def _():
            for item in copies(j, 0):
                item.wait_send()

        @pl.when((j <= z) & (z < chans - 1))
        def _():
            for item in copies(j, 1):
                item.wait_send()

        for item in copies(j, 2):
            item.wait_send()
        return carry

    lax.fori_loop(0, chans, drain, 0)

    def drain_parts(d, carry):
        for o in range(1, wins):
            part_copy(d, o).wait_send()
        return carry

    lax.fori_loop(0, dist, drain_parts, 0)
    for o in range(1, wins):
        image_copy(o).wait_send()

    def drain_gram(o, carry):
        gram_copy(o, False).wait_send()
        return carry

    lax.fori_loop(1, peers, drain_gram, 0)


def body(chans, wins, records, lag_weights, probes):
    rows, width = records.shape
    k = probes.shape[1]
    dist = chans // 2 + 1
    part_width = 2 * rows // wins
    dma = pltpu.SemaphoreType.DMA
    return pl.pallas_call(
        functools.partial(kernel, chans, wins, width * wins),
        out_shape=(
            jax.ShapeDtypeStruct((dist, rows, part_width), jnp.bfloat16),
            jax.ShapeDtypeStruct((rows, k), jnp.float32),
        ),
        in_specs=[pl.BlockSpec(memory_space=pltpu.VMEM)] * 3,
        out_specs=(pl.BlockSpec(memory_space=pltpu.VMEM),) * 2,
        scratch_shapes=[
            pltpu.VMEM((chans, 2 * rows, width), jnp.bfloat16),
            pltpu.VMEM((chans, 2 * rows, k), jnp.bfloat16),
            pltpu.VMEM((rows, width + 2 * LANES), jnp.bfloat16),
            pltpu.VMEM((rows, width), jnp.bfloat16),
            pltpu.VMEM((dist, wins, rows, part_width), jnp.float32),
            pltpu.VMEM((dist, wins, rows, part_width), jnp.bfloat16),
            pltpu.VMEM((dist, wins, rows, part_width), jnp.bfloat16),
            pltpu.VMEM((rows, k), jnp.float32),
            pltpu.VMEM((wins, rows, k), jnp.float32),
            pltpu.VMEM((2 * chans, k, k), jnp.float32),
            dma((2,)),
            dma((chans, 3)), dma((chans, 2)),
            dma((chans, 3)), dma((chans, 2)),
            dma((2,)), dma((2,)),
            dma((dist, wins)), dma((dist, wins)),
            dma((wins,)), dma((wins,)),
            dma((2 * chans,)), dma((2 * chans,)),
        ],
        compiler_params=pltpu.CompilerParams(
            collective_id=0, has_side_effects=True, vmem_limit_bytes=48 * 1024 * 1024
        ),
    )(records, lag_weights.reshape(1, -1), probes)


def solution(mesh):
    return jax.shard_map(
        functools.partial(body, mesh.shape["chan"], mesh.shape["win"]),
        mesh=mesh,
        in_specs=(P(("groups", "chan", "sub"), "win"), P(), P(("groups", "chan", "sub"), None)),
        out_specs=(P(None, ("groups", "chan", "sub"), "win"), P(("groups", "chan", "sub"), None)),
        check_vma=False,
    )
```

time: 233 us -> 46.2 us (0.20); the launches traced: 229 us -> 46 us
  other arithmetic: 69.5 us -> 0 us
  waiting for transfers between devices: 58.9 us -> 0 us
  Pallas kernels: 0 us -> 42.2 us
  local copies, waits for them, and re-layouts: 40.6 us -> 3.11 us
  blocking collectives: 33 us -> 0 us
  between operations: 13.9 us -> 0.66 us
  matrix products: 5.77 us -> 0 us
  starting transfers between devices: 5.35 us -> 0 us
    psum x1 -> x0, waiting for transfers between devices: 55.2 us -> none  [body(): window_products = lax.psum(local_products, ('chan', 'sub'))]
    add x65 -> x0, other arithmetic: 53.2 us -> none  [add_lag(): return running + weights[lag_index] * window]
    pallas_call x0 -> x1, Pallas kernels: none -> 42.2 us  [body(): pl.pallas_call(functools.partial(kernel, chans, wins, width * wins), out_...]
    dynamic_slice x65 -> x0, local copies, waits for them, and re-layouts: 38.1 us -> none  [add_lag(): return running + weights[lag_index] * window]
    psum x2 -> x0, blocking collectives: 33 us -> none  [the longest x1 26.7 us: body(): gram_matrix = lax.psum(local_gram, ('chan', 'sub')) / (CB * chan_count)]
    another operation x5 -> x0, other arithmetic: 12.1 us -> none  [the longest x3 6.52 us: body(): factor = jnp.linalg.cholesky(gram_matrix)]
    ppermute x2 -> x0, starting transfers between devices: 5.23 us -> none  [the longest x1 3.94 us: extended(): lax.ppermute(lax.slice_in_dim(block, block.shape[dim] - width, None, axis...]
    dot_general x4 -> x0, matrix products: 4.9 us -> none  [the longest x1 2.13 us: body(): lax.dot_general(records, lax.all_gather(filtered, ('chan', 'sub'), axis=0...]
  transfers between devices with their start and end apart: 5 -> 0, of which waited for: 3 -> 0; matrix products, arithmetic and copies ran while one was open for 7% -> 0% of each run, Pallas kernels for 0% -> 0%
where the time goes in v1:
time: 46.2 us; the launch traced here: 46 us
  Pallas kernels  42.2 us (91%)
  local copies, waits for them, and re-layouts  3.11 us (7%)
  between operations  0.66 us (1%)
    pallas_call x1, Pallas kernels, body(): pl.pallas_call(functools.partial(kernel, chans, wins, width * wins), out_...  42.2 us
    unnamed x6, local copies, waits for them, and re-layouts  2.41 us

profile of v1, /device:TPU:1, one launch (start us, length us, event | category | flops | bytes accessed | tf_op | source)
XLA Modules:
  0.0 46.0 jit_solution(12860241230586438951)
XLA Ops:
  0.6 0.0 copy-start.1
  0.6 0.8 %copy.5.p_ref = bf16[128,64]{1,0:T(8,128)(2,1)S(1)} copy(bf16[128,64]{0,1:T(8,128)(2,1)} %param.5) | data formatting | bytes 32768 | tf_op args[2]
  1.5 0.0 copy-done.1
  1.5 0.0 copy-start
  1.5 0.9 %copy-done = bf16[128,896]{1,0:T(8,128)(2,1)S(1)} copy-done((bf16[128,896]{1,0:T(8,128)(2,1)S(1)}, bf16[128,896]{1,0:T(8,128)(2,1)}, u32[]{:S(2)}) %copy-start) | copy-done | bytes 229400
  2.4 42.2 %shard_map.50 = (bf16[3,128,128]{2,1,0:T(8,128)(2,1)S(1)}, f32[128,64]{1,0:T(8,128)S(1)}) custom-call(bf16[128,896]{1,0:T(8,128)(2,1)S(1)} %copy-done, f32[1,65]{1,0:T(1,128)S(1)} %bitcast.1, bf16[128,64]{1,0:T(8,128)(2,1)S(1)} %copy.5.p_ref), custom_call_target="tpu_custom_call" | custom-call | tf_op jit(solution)/shard_map/pallas_call | solution.py:393
  44.6 0.7 %copy.6 = f32[128,64]{0,1:T(8,128)} copy(f32[128,64]{1,0:T(8,128)S(1)} %get-tuple-element.3) | data formatting | bytes 65536 | tf_op jit(solution)/shard_map/pallas_call | solution.py:393
  45.3 0.6 %copy.8 = bf16[3,128,128]{2,1,0:T(8,128)(2,1)} copy(bf16[3,128,128]{2,1,0:T(8,128)(2,1)S(1)} %get-tuple-element.6) | data formatting | bytes 196608
Async XLA Ops:
  0.6 0.8 %copy-start.1 = (f32[65]{0:T(128)S(1)}, f32[65]{0:T(128)}, u32[]{:S(2)}) copy-start(f32[65]{0:T(128)} %param.4) | copy-start | bytes 784
  1.5 0.9 %copy-start = (bf16[128,896]{1,0:T(8,128)(2,1)S(1)}, bf16[128,896]{1,0:T(8,128)(2,1)}, u32[]{:S(2)}) copy-start(bf16[128,896]{1,0:T(8,128)(2,1)} %r_ref.1) | copy-start | bytes 688132

commit v2 on v1

--- a/solution.py
+++ b/solution.py
@@ -10,6 +10,7 @@
 MESH = pl.DeviceIdType.MESH
 MAXLAG = 32
 LANES = 128
+PIECE = 16
 HIGHEST = lax.Precision.HIGHEST
 
 
@@ -55,8 +56,8 @@
     chans, wins, samples,
     r_ref, w_ref, p_ref,
     cov_ref, sub_ref,
-    g, pg, ext, filt, part, sendp, recvp, im, ib, gb,
-    local_sem, r_send, r_recv, p_send, p_recv, h_send, h_recv,
+    g, ext, filt, part, sendp, recvp, zl, zr, zs, ib, gb,
+    local_sem, r_send, r_recv, z_send, z_recv, y_send, y_recv, h_send, h_recv,
     c_send, c_recv, i_send, i_recv, g_send, g_recv,
 ):
     z = lax.axis_index("chan")
@@ -68,6 +69,9 @@
     peers = 2 * chans
     me = z * 2 + s
     other = 1 - s
+    half = chans // 2
+    pieces = zs.shape[0]
+    owners = [((q * chans) // pieces, q % 2) for q in range(pieces)]
 
     barrier = pltpu.get_barrier_semaphore()
 
@@ -83,6 +87,11 @@
         pl.semaphore_signal(
             barrier, inc=1, device_id={"win": lax.rem(w + o, wins)}, device_id_type=MESH
         )
+    moments = lax.dot_general(
+        p_ref[...], r_ref[...], (((0,), (0,)), ((), ())), preferred_element_type=jnp.float32
+    )
+    for q in range(pieces):
+        zl[q] = moments[q * PIECE : (q + 1) * PIECE, :].astype(zl.dtype)
     pl.semaphore_wait(barrier, peers - 1 + wins - 1)
 
     def rows_of(sub):
@@ -93,38 +102,76 @@
             return {"sub": other}
         return {"chan": z + (1 if way == 1 else -1)}
 
-    def copies(j, way, source_r=None, source_p=None):
+    def copy(j, way, own=False):
         place = rows_of(s)
-        return [
-            pltpu.make_async_remote_copy(
-                src_ref=p_ref if source_p is not None else pg.at[j, place],
-                dst_ref=pg.at[j, place],
-                send_sem=p_send.at[j, way],
-                recv_sem=p_recv.at[j, s],
-                device_id=to(way),
-                device_id_type=MESH,
-            ),
-            pltpu.make_async_remote_copy(
-                src_ref=r_ref if source_r is not None else g.at[j, place],
-                dst_ref=g.at[j, place],
-                send_sem=r_send.at[j, way],
-                recv_sem=r_recv.at[j, s],
-                device_id=to(way),
-                device_id_type=MESH,
-            ),
-        ]
+        return pltpu.make_async_remote_copy(
+            src_ref=r_ref if own else g.at[j, place],
+            dst_ref=g.at[j, place],
+            send_sem=r_send.at[j, way],
+            recv_sem=r_recv.at[j, s],
+            device_id=to(way),
+            device_id_type=MESH,
+        )
+
+    def goes_down(j):
+        return (z > 0) & (j >= z) & (j - z < half)
+
+    def goes_up(j):
+        return (z < chans - 1) & (j <= z) & (j + half < chans)
+
+    def used(j):
+        return lax.rem(j - z + chans, chans) < dist
 
     def landed(j, sub):
         place = rows_of(sub)
-        for buffer, sends, receives in ((pg, p_send, p_recv), (g, r_send, r_recv)):
-            pltpu.make_async_remote_copy(
-                src_ref=buffer.at[j, place],
-                dst_ref=buffer.at[j, place],
-                send_sem=sends.at[j, 2],
-                recv_sem=receives.at[j, sub],
-                device_id={"sub": other},
-                device_id_type=MESH,
-            ).wait_recv()
+        pltpu.make_async_remote_copy(
+            src_ref=g.at[j, place],
+            dst_ref=g.at[j, place],
+            send_sem=r_send.at[j, 2],
+            recv_sem=r_recv.at[j, sub],
+            device_id={"sub": other},
+            device_id_type=MESH,
+        ).wait_recv()
+
+    def piece_copy(q):
+        return pltpu.make_async_remote_copy(
+            src_ref=zl.at[q],
+            dst_ref=zr.at[me],
+            send_sem=z_send.at[q],
+            recv_sem=z_recv.at[me],
+            device_id={"chan": owners[q][0], "sub": owners[q][1]},
+            device_id_type=MESH,
+        )
+
+    def owns(q):
+        return (z == owners[q][0]) & (s == owners[q][1])
+
+    def peer(o):
+        t = lax.rem(me + o, peers)
+        return t, {"chan": t // 2, "sub": t % 2}
+
+    def piece_landed(o, carry):
+        t, device = peer(o)
+        pltpu.make_async_remote_copy(
+            src_ref=zr.at[t],
+            dst_ref=zr.at[t],
+            send_sem=z_send.at[0],
+            recv_sem=z_recv.at[t],
+            device_id=device,
+            device_id_type=MESH,
+        ).wait_recv()
+        return carry
+
+    def sum_copy(q, o):
+        t, device = peer(o)
+        return pltpu.make_async_remote_copy(
+            src_ref=zs.at[q],
+            dst_ref=zs.at[q],
+            send_sem=y_send.at[t],
+            recv_sem=y_recv.at[q],
+            device_id=device,
+            device_id_type=MESH,
+        )
 
     def halo(up):
         source = pl.ds(width - LANES, LANES) if up else pl.ds(0, LANES)
@@ -138,9 +185,11 @@
             device_id_type=MESH,
         )
 
-    def start_all(items):
-        for item in items:
-            item.start()
+    for q in range(pieces):
+
+        @pl.when(jnp.logical_not(owns(q)))
+        def _(q=q):
+            piece_copy(q).start()
 
     @pl.when(w < wins - 1)
     def _():
@@ -150,20 +199,17 @@
     def _():
         halo(False).start()
 
-    @pl.when(z < chans - 1)
-    def _():
-        start_all(copies(z, 1, True, True))
-
-    @pl.when(z > 0)
-    def _():
-        start_all(copies(z, 0, True, True))
-
-    start_all(copies(z, 2, True, True))
-    local = [
-        pltpu.make_async_copy(p_ref, pg.at[z, rows_of(s)], local_sem.at[0]),
-        pltpu.make_async_copy(r_ref, g.at[z, rows_of(s)], local_sem.at[1]),
-    ]
-    start_all(local)
+    @pl.when(goes_up(z))
+    def _():
+        copy(z, 1, True).start()
+
+    @pl.when(goes_down(z))
+    def _():
+        copy(z, 0, True).start()
+
+    copy(z, 2, True).start()
+    local = pltpu.make_async_copy(r_ref, g.at[z, rows_of(s)], local_sem.at[0])
+    local.start()
 
     @pl.when(w == 0)
     def _():
@@ -174,7 +220,6 @@
         ext[:, LANES + width :] = jnp.zeros((rows, LANES), ext.dtype)
 
     ext[:, LANES : LANES + width] = r_ref[...]
-    im[...] = jnp.zeros_like(im)
     band_high, band_low = halves(banded(w_ref[...]))
 
     @pl.when(w > 0)
@@ -188,7 +233,27 @@
     for b in range(width // LANES):
         window = ext[:, b * LANES : (b + 3) * LANES]
         value = dot_rows(window, band_high) + dot_rows(window, band_low)
-        filt[:, b * LANES : (b + 1) * LANES] = value.astype(filt.dtype)
+        high, low = halves(value)
+        filt[0, :, b * LANES : (b + 1) * LANES] = high
+        filt[1, :, b * LANES : (b + 1) * LANES] = low
+
+    for q in range(pieces):
+
+        @pl.when(owns(q))
+        def _(q=q):
+            lax.fori_loop(1, peers, piece_landed, 0)
+            zr[me] = zl[q]
+            total = lax.fori_loop(
+                1, peers, lambda t, run: run + zr[t].astype(jnp.float32),
+                zr[0].astype(jnp.float32),
+            )
+            zs[q] = total.astype(zs.dtype)
+
+            def send(o, carry):
+                sum_copy(q, o).start()
+                return carry
+
+            lax.fori_loop(1, peers, send, 0)
 
     def part_copy(d, o):
         t = lax.rem(w + o, wins)
@@ -202,66 +267,62 @@
         )
 
     def block(j):
-        value = dot_rows(filt[...], g[j])
+        value = dot_rows(filt[0], g[j]) + dot_rows(filt[1], g[j])
         d = lax.rem(j - z + chans, chans)
-        high, low = halves(value)
-        probes = pg[j]
-        im[...] += jnp.dot(high, probes, preferred_element_type=jnp.float32) + jnp.dot(
-            low, probes, preferred_element_type=jnp.float32
-        )
-
-        @pl.when(d < dist)
-        def _():
-            for t in range(wins):
-                piece = value[:, t * part_width : (t + 1) * part_width]
-                part[d, t] = piece
-                sendp[d, t] = piece.astype(sendp.dtype)
-            for o in range(1, wins):
-                part_copy(d, o).start()
-
-    for item in local:
-        item.wait()
-    landed(z, other)
-    block(z)
-
-    def hop(h, carry):
+        for t in range(wins):
+            piece = value[:, t * part_width : (t + 1) * part_width]
+            part[d, t] = piece
+            sendp[d, t] = piece.astype(sendp.dtype)
+        for o in range(1, wins):
+            part_copy(d, o).start()
+
+    def forward(h):
         above, below = z + h, z - h
 
-        @pl.when(above < chans)
+        @pl.when((above < chans) & (h <= half))
         def _():
             landed(above, s)
 
-            @pl.when(z > 0)
+            @pl.when(goes_down(above))
             def _():
-                start_all(copies(above, 0))
-
-            start_all(copies(above, 2))
-
-        @pl.when(below >= 0)
+                copy(above, 0).start()
+
+            copy(above, 2).start()
+
+        @pl.when((below >= 0) & (below + half < chans))
         def _():
             landed(below, s)
 
-            @pl.when(z < chans - 1)
+            @pl.when(goes_up(below))
             def _():
-                start_all(copies(below, 1))
-
-            start_all(copies(below, 2))
-
-        @pl.when(above < chans)
+                copy(below, 1).start()
+
+            @pl.when(used(below))
+            def _():
+                copy(below, 2).start()
+
+    def take(h):
+        above, below = z + h, z - h
+
+        @pl.when((above < chans) & (h <= half))
         def _():
             landed(above, other)
             block(above)
 
-        @pl.when(below >= 0)
+        @pl.when((below >= 0) & (below + half < chans) & (h >= half))
         def _():
             landed(below, other)
             block(below)
 
-        return carry
-
-    lax.fori_loop(1, chans, hop, 0)
-
-    ib[w] = im[...]
+    forward(1)
+    for q in range(pieces):
+
+        @pl.when(jnp.logical_not(owns(q)))
+        def _(q=q):
+            sum_copy(q, 1).wait_recv()
+
+    moments = zs[...].reshape(pieces * PIECE, width)
+    ib[w] = dot_rows(filt[0], moments) + dot_rows(filt[1], moments)
 
     def image_copy(o):
         t = lax.rem(w + o, wins)
@@ -287,6 +348,10 @@
 
     for o in range(1, wins):
         image_copy(o).start()
+    local.wait()
+    landed(z, other)
+    block(z)
+    take(1)
     for o in range(1, wins):
         image_landed(o).wait_recv()
     images = ib[0]
@@ -315,6 +380,22 @@
         return carry
 
     lax.fori_loop(1, peers, gram_start, 0)
+
+    def hop(h, carry):
+        forward(h)
+        take(h)
+        return carry
+
+    lax.fori_loop(2, chans, hop, 0)
+
+    def gram_landed(o, carry):
+        gram_copy(o, True).wait_recv()
+        return carry
+
+    lax.fori_loop(1, peers, gram_landed, 0)
+    gram = lax.fori_loop(1, peers, lambda t, total: total + gb[t], gb[0])
+    inverse = inverse_factor(gram * (1.0 / (rows * peers)))
+    sub_ref[...] = dot_rows(images, inverse, HIGHEST)
 
     def finish(d, carry):
         total = part[d, w]
@@ -334,15 +415,6 @@
 
     lax.fori_loop(0, dist, finish, 0)
 
-    def gram_landed(o, carry):
-        gram_copy(o, True).wait_recv()
-        return carry
-
-    lax.fori_loop(1, peers, gram_landed, 0)
-    gram = lax.fori_loop(1, peers, lambda t, total: total + gb[t], gb[0])
-    inverse = inverse_factor(gram * (1.0 / (rows * peers)))
-    sub_ref[...] = dot_rows(images, inverse, HIGHEST)
-
     @pl.when(w < wins - 1)
     def _():
         halo(True).wait_send()
@@ -351,19 +423,33 @@
     def _():
         halo(False).wait_send()
 
+    for q in range(pieces):
+
+        @pl.when(jnp.logical_not(owns(q)))
+        def _(q=q):
+            piece_copy(q).wait_send()
+
+        @pl.when(owns(q))
+        def _(q=q):
+            def sent(o, carry):
+                sum_copy(q, o).wait_send()
+                return carry
+
+            lax.fori_loop(1, peers, sent, 0)
+
     def drain(j, carry):
-        @pl.when((j >= z) & (z > 0))
-        def _():
-            for item in copies(j, 0):
-                item.wait_send()
-
-        @pl.when((j <= z) & (z < chans - 1))
-        def _():
-            for item in copies(j, 1):
-                item.wait_send()
-
-        for item in copies(j, 2):
-            item.wait_send()
+        @pl.when(goes_down(j))
+        def _():
+            copy(j, 0).wait_send()
+
+        @pl.when(goes_up(j))
+        def _():
+            copy(j, 1).wait_send()
+
+        @pl.when(used(j))
+        def _():
+            copy(j, 2).wait_send()
+
         return carry
 
     lax.fori_loop(0, chans, drain, 0)
@@ -400,18 +486,20 @@
         out_specs=(pl.BlockSpec(memory_space=pltpu.VMEM),) * 2,
         scratch_shapes=[
             pltpu.VMEM((chans, 2 * rows, width), jnp.bfloat16),
-            pltpu.VMEM((chans, 2 * rows, k), jnp.bfloat16),
             pltpu.VMEM((rows, width + 2 * LANES), jnp.bfloat16),
-            pltpu.VMEM((rows, width), jnp.bfloat16),
+            pltpu.VMEM((2, rows, width), jnp.bfloat16),
             pltpu.VMEM((dist, wins, rows, part_width), jnp.float32),
             pltpu.VMEM((dist, wins, rows, part_width), jnp.bfloat16),
             pltpu.VMEM((dist, wins, rows, part_width), jnp.bfloat16),
-            pltpu.VMEM((rows, k), jnp.float32),
+            pltpu.VMEM((k // PIECE, PIECE, width), jnp.bfloat16),
+            pltpu.VMEM((2 * chans, PIECE, width), jnp.bfloat16),
+            pltpu.VMEM((k // PIECE, PIECE, width), jnp.bfloat16),
             pltpu.VMEM((wins, rows, k), jnp.float32),
             pltpu.VMEM((2 * chans, k, k), jnp.float32),
-            dma((2,)),
+            dma((1,)),
             dma((chans, 3)), dma((chans, 2)),
-            dma((chans, 3)), dma((chans, 2)),
+            dma((k // PIECE,)), dma((2 * chans,)),
+            dma((2 * chans,)), dma((k // PIECE,)),
             dma((2,)), dma((2,)),
             dma((dist, wins)), dma((dist, wins)),
             dma((wins,)), dma((wins,)),

time: 46.2 us -> 40.4 us (0.87)
  the two profiles are of different devices: /device:TPU:1 before, /device:TPU:31 now
where the time goes in v2:
time: 40.4 us; the launch traced here: 40.1 us
  Pallas kernels  36.4 us (90%)
  local copies, waits for them, and re-layouts  3.11 us (8%)
  between operations  0.66 us (2%)
    pallas_call x1, Pallas kernels, body(): pl.pallas_call(functools.partial(kernel, chans, wins, width * wins), out_...  36.4 us
    unnamed x6, local copies, waits for them, and re-layouts  2.41 us

profile of v2, /device:TPU:31, one launch (start us, length us, event | category | flops | bytes accessed | tf_op | source)
XLA Modules:
  0.0 40.1 jit_solution(3874171472911394110)
XLA Ops:
  0.6 0.0 copy-start.1
  0.6 0.8 %copy.5.p_ref = bf16[128,64]{1,0:T(8,128)(2,1)S(1)} copy(bf16[128,64]{0,1:T(8,128)(2,1)} %param.5) | data formatting | bytes 32768 | tf_op args[2]
  1.5 0.0 copy-done.1
  1.5 0.0 copy-start
  1.5 0.9 %copy-done = bf16[128,896]{1,0:T(8,128)(2,1)S(1)} copy-done((bf16[128,896]{1,0:T(8,128)(2,1)S(1)}, bf16[128,896]{1,0:T(8,128)(2,1)}, u32[]{:S(2)}) %copy-start) | copy-done | bytes 229400
  2.4 36.4 %shard_map.50 = (bf16[3,128,128]{2,1,0:T(8,128)(2,1)S(1)}, f32[128,64]{1,0:T(8,128)S(1)}) custom-call(bf16[128,896]{1,0:T(8,128)(2,1)S(1)} %copy-done, f32[1,65]{1,0:T(1,128)S(1)} %bitcast.1, bf16[128,64]{1,0:T(8,128)(2,1)S(1)} %copy.5.p_ref), custom_call_target="tpu_custom_call" | custom-call | tf_op jit(solution)/shard_map/pallas_call | solution.py:479
  38.8 0.7 %copy.6 = f32[128,64]{0,1:T(8,128)} copy(f32[128,64]{1,0:T(8,128)S(1)} %get-tuple-element.3) | data formatting | bytes 65536 | tf_op jit(solution)/shard_map/pallas_call | solution.py:479
  39.5 0.6 %copy.8 = bf16[3,128,128]{2,1,0:T(8,128)(2,1)} copy(bf16[3,128,128]{2,1,0:T(8,128)(2,1)S(1)} %get-tuple-element.6) | data formatting | bytes 196608
Async XLA Ops:
  0.6 0.8 %copy-start.1 = (f32[65]{0:T(128)S(1)}, f32[65]{0:T(128)}, u32[]{:S(2)}) copy-start(f32[65]{0:T(128)} %param.4) | copy-start | bytes 784
  1.5 0.9 %copy-start = (bf16[128,896]{1,0:T(8,128)(2,1)S(1)}, bf16[128,896]{1,0:T(8,128)(2,1)}, u32[]{:S(2)}) copy-start(bf16[128,896]{1,0:T(8,128)(2,1)} %r_ref.1) | copy-start | bytes 688132

commit v3 on v2

--- a/solution.py
+++ b/solution.py
@@ -11,6 +11,7 @@
 MAXLAG = 32
 LANES = 128
 PIECE = 16
+CHUNKS = 4
 HIGHEST = lax.Precision.HIGHEST
 
 
@@ -73,6 +74,11 @@
     pieces = zs.shape[0]
     owners = [((q * chans) // pieces, q % 2) for q in range(pieces)]
 
+    def rows_of(sub):
+        return pl.ds(pl.multiple_of(sub * rows, rows), rows)
+
+    local = pltpu.make_async_copy(r_ref, g.at[z, rows_of(s)], local_sem.at[0])
+    local.start()
     barrier = pltpu.get_barrier_semaphore()
 
     def greet(o, carry):
@@ -87,28 +93,31 @@
         pl.semaphore_signal(
             barrier, inc=1, device_id={"win": lax.rem(w + o, wins)}, device_id_type=MESH
         )
+    local.wait()
     moments = lax.dot_general(
-        p_ref[...], r_ref[...], (((0,), (0,)), ((), ())), preferred_element_type=jnp.float32
+        p_ref[...], g[z, rows_of(s), :], (((1,), (0,)), ((), ())),
+        preferred_element_type=jnp.float32,
     )
     for q in range(pieces):
         zl[q] = moments[q * PIECE : (q + 1) * PIECE, :].astype(zl.dtype)
     pl.semaphore_wait(barrier, peers - 1 + wins - 1)
 
-    def rows_of(sub):
-        return pl.ds(pl.multiple_of(sub * rows, rows), rows)
+    def chunk_of(sub, c):
+        size = rows // CHUNKS
+        return pl.ds(pl.multiple_of(sub * rows + c * size, size), size)
 
     def to(way):
         if way == 2:
             return {"sub": other}
         return {"chan": z + (1 if way == 1 else -1)}
 
-    def copy(j, way, own=False):
-        place = rows_of(s)
-        return pltpu.make_async_remote_copy(
-            src_ref=r_ref if own else g.at[j, place],
+    def copy(j, way, c):
+        place = chunk_of(s, c)
+        return pltpu.make_async_remote_copy(
+            src_ref=g.at[j, place],
             dst_ref=g.at[j, place],
-            send_sem=r_send.at[j, way],
-            recv_sem=r_recv.at[j, s],
+            send_sem=r_send.at[j, way, c],
+            recv_sem=r_recv.at[j, s, c],
             device_id=to(way),
             device_id_type=MESH,
         )
@@ -122,13 +131,13 @@
     def used(j):
         return lax.rem(j - z + chans, chans) < dist
 
-    def landed(j, sub):
-        place = rows_of(sub)
+    def landed(j, sub, c):
+        place = chunk_of(sub, c)
         pltpu.make_async_remote_copy(
             src_ref=g.at[j, place],
             dst_ref=g.at[j, place],
-            send_sem=r_send.at[j, 2],
-            recv_sem=r_recv.at[j, sub],
+            send_sem=r_send.at[j, 2, c],
+            recv_sem=r_recv.at[j, sub, c],
             device_id={"sub": other},
             device_id_type=MESH,
         ).wait_recv()
@@ -177,7 +186,7 @@
         source = pl.ds(width - LANES, LANES) if up else pl.ds(0, LANES)
         target = pl.ds(0, LANES) if up else pl.ds(width + LANES, LANES)
         return pltpu.make_async_remote_copy(
-            src_ref=r_ref.at[:, source],
+            src_ref=g.at[z, rows_of(s), source],
             dst_ref=ext.at[:, target],
             send_sem=h_send.at[int(up)],
             recv_sem=h_recv.at[int(up)],
@@ -185,31 +194,32 @@
             device_id_type=MESH,
         )
 
+    @pl.when(w < wins - 1)
+    def _():
+        halo(True).start()
+
+    @pl.when(w > 0)
+    def _():
+        halo(False).start()
+
     for q in range(pieces):
 
         @pl.when(jnp.logical_not(owns(q)))
         def _(q=q):
             piece_copy(q).start()
 
-    @pl.when(w < wins - 1)
-    def _():
-        halo(True).start()
-
-    @pl.when(w > 0)
-    def _():
-        halo(False).start()
-
-    @pl.when(goes_up(z))
-    def _():
-        copy(z, 1, True).start()
-
-    @pl.when(goes_down(z))
-    def _():
-        copy(z, 0, True).start()
-
-    copy(z, 2, True).start()
-    local = pltpu.make_async_copy(r_ref, g.at[z, rows_of(s)], local_sem.at[0])
-    local.start()
+    for c in range(CHUNKS):
+
+        @pl.when(goes_up(z))
+        def _(c=c):
+            copy(z, 1, c).start()
+
+        @pl.when(goes_down(z))
+        def _(c=c):
+            copy(z, 0, c).start()
+
+    for c in range(CHUNKS):
+        copy(z, 2, c).start()
 
     @pl.when(w == 0)
     def _():
@@ -219,7 +229,7 @@
     def _():
         ext[:, LANES + width :] = jnp.zeros((rows, LANES), ext.dtype)
 
-    ext[:, LANES : LANES + width] = r_ref[...]
+    ext[:, LANES : LANES + width] = g[z, rows_of(s), :]
     band_high, band_low = halves(banded(w_ref[...]))
 
     @pl.when(w > 0)
@@ -276,42 +286,48 @@
         for o in range(1, wins):
             part_copy(d, o).start()
 
-    def forward(h):
+    def forward_chunk(h, c):
         above, below = z + h, z - h
 
         @pl.when((above < chans) & (h <= half))
         def _():
-            landed(above, s)
+            landed(above, s, c)
 
             @pl.when(goes_down(above))
             def _():
-                copy(above, 0).start()
-
-            copy(above, 2).start()
+                copy(above, 0, c).start()
+
+            copy(above, 2, c).start()
 
         @pl.when((below >= 0) & (below + half < chans))
         def _():
-            landed(below, s)
+            landed(below, s, c)
 
             @pl.when(goes_up(below))
             def _():
-                copy(below, 1).start()
+                copy(below, 1, c).start()
 
             @pl.when(used(below))
             def _():
-                copy(below, 2).start()
+                copy(below, 2, c).start()
+
+    def forward(h):
+        for c in range(CHUNKS):
+            forward_chunk(h, c)
 
     def take(h):
         above, below = z + h, z - h
 
         @pl.when((above < chans) & (h <= half))
         def _():
-            landed(above, other)
+            for c in range(CHUNKS):
+                landed(above, other, c)
             block(above)
 
         @pl.when((below >= 0) & (below + half < chans) & (h >= half))
         def _():
-            landed(below, other)
+            for c in range(CHUNKS):
+                landed(below, other, c)
             block(below)
 
     forward(1)
@@ -322,7 +338,7 @@
             sum_copy(q, 1).wait_recv()
 
     moments = zs[...].reshape(pieces * PIECE, width)
-    ib[w] = dot_rows(filt[0], moments) + dot_rows(filt[1], moments)
+    ib[w] = dot_rows(moments, filt[0]) + dot_rows(moments, filt[1])
 
     def image_copy(o):
         t = lax.rem(w + o, wins)
@@ -348,8 +364,8 @@
 
     for o in range(1, wins):
         image_copy(o).start()
-    local.wait()
-    landed(z, other)
+    for c in range(CHUNKS):
+        landed(z, other, c)
     block(z)
     take(1)
     for o in range(1, wins):
@@ -358,10 +374,9 @@
     for t in range(1, wins):
         images = images + ib[t]
     images = images * (1.0 / samples)
-    gb[me] = lax.dot_general(
-        images, images, (((0,), (0,)), ((), ())), precision=HIGHEST,
-        preferred_element_type=jnp.float32,
-    )
+    gram = dot_rows(images, images, HIGHEST)
+    k = gram.shape[0]
+    gb[me] = jnp.concatenate([gram[: k // 2], gram[k // 2 :]], axis=1)
 
     def gram_copy(o, slot):
         t = lax.rem(me + o, peers)
@@ -394,8 +409,9 @@
 
     lax.fori_loop(1, peers, gram_landed, 0)
     gram = lax.fori_loop(1, peers, lambda t, total: total + gb[t], gb[0])
+    gram = jnp.concatenate([gram[:, :k], gram[:, k:]], axis=0)
     inverse = inverse_factor(gram * (1.0 / (rows * peers)))
-    sub_ref[...] = dot_rows(images, inverse, HIGHEST)
+    sub_ref[...] = jnp.dot(inverse, images, precision=HIGHEST)
 
     def finish(d, carry):
         total = part[d, w]
@@ -438,17 +454,19 @@
             lax.fori_loop(1, peers, sent, 0)
 
     def drain(j, carry):
-        @pl.when(goes_down(j))
-        def _():
-            copy(j, 0).wait_send()
-
-        @pl.when(goes_up(j))
-        def _():
-            copy(j, 1).wait_send()
-
-        @pl.when(used(j))
-        def _():
-            copy(j, 2).wait_send()
+        for c in range(CHUNKS):
+
+            @pl.when(goes_down(j))
+            def _(c=c):
+                copy(j, 0, c).wait_send()
+
+            @pl.when(goes_up(j))
+            def _(c=c):
+                copy(j, 1, c).wait_send()
+
+            @pl.when(used(j))
+            def _(c=c):
+                copy(j, 2, c).wait_send()
 
         return carry
 
@@ -476,13 +494,17 @@
     dist = chans // 2 + 1
     part_width = 2 * rows // wins
     dma = pltpu.SemaphoreType.DMA
-    return pl.pallas_call(
+    covariance, transposed = pl.pallas_call(
         functools.partial(kernel, chans, wins, width * wins),
         out_shape=(
             jax.ShapeDtypeStruct((dist, rows, part_width), jnp.bfloat16),
-            jax.ShapeDtypeStruct((rows, k), jnp.float32),
+            jax.ShapeDtypeStruct((k, rows), jnp.float32),
         ),
-        in_specs=[pl.BlockSpec(memory_space=pltpu.VMEM)] * 3,
+        in_specs=[
+            pl.BlockSpec(memory_space=pltpu.HBM),
+            pl.BlockSpec(memory_space=pltpu.VMEM),
+            pl.BlockSpec(memory_space=pltpu.VMEM),
+        ],
         out_specs=(pl.BlockSpec(memory_space=pltpu.VMEM),) * 2,
         scratch_shapes=[
             pltpu.VMEM((chans, 2 * rows, width), jnp.bfloat16),
@@ -494,10 +516,10 @@
             pltpu.VMEM((k // PIECE, PIECE, width), jnp.bfloat16),
             pltpu.VMEM((2 * chans, PIECE, width), jnp.bfloat16),
             pltpu.VMEM((k // PIECE, PIECE, width), jnp.bfloat16),
-            pltpu.VMEM((wins, rows, k), jnp.float32),
-            pltpu.VMEM((2 * chans, k, k), jnp.float32),
+            pltpu.VMEM((wins, k, rows), jnp.float32),
+            pltpu.VMEM((2 * chans, k // 2, 2 * k), jnp.float32),
             dma((1,)),
-            dma((chans, 3)), dma((chans, 2)),
+            dma((chans, 3, CHUNKS)), dma((chans, 2, CHUNKS)),
             dma((k // PIECE,)), dma((2 * chans,)),
             dma((2 * chans,)), dma((k // PIECE,)),
             dma((2,)), dma((2,)),
@@ -508,7 +530,8 @@
         compiler_params=pltpu.CompilerParams(
             collective_id=0, has_side_effects=True, vmem_limit_bytes=48 * 1024 * 1024
         ),
-    )(records, lag_weights.reshape(1, -1), probes)
+    )(records, lag_weights.reshape(1, -1), probes.T)
+    return covariance, transposed.T
 
 
 def solution(mesh):

time: 40.4 us -> 38.6 us (0.955)
  the two profiles are of different devices: /device:TPU:31 before, /device:TPU:29 now
where the time goes in v3:
time: 38.6 us; the launch traced here: 38.3 us
  Pallas kernels  34.1 us (88%)
  local copies, waits for them, and re-layouts  3.56 us (9%)
  between operations  0.65 us (2%)
    pallas_call x1, Pallas kernels, body(): pl.pallas_call(functools.partial(kernel, chans, wins, width * wins), out_...  34.1 us
    unnamed x8, local copies, waits for them, and re-layouts  3.56 us

profile of v3, /device:TPU:29, one launch (start us, length us, event | category | flops | bytes accessed | tf_op | source)
XLA Modules:
  0.0 38.3 jit_solution(10204524714075563592)
XLA Ops:
  0.6 0.0 copy-start.2
  0.6 0.6 %copy-done.2 = f32[65]{0:T(128)S(1)} copy-done((f32[65]{0:T(128)S(1)}, f32[65]{0:T(128)}, u32[]{:S(2)}) %copy-start.2) | copy-done | bytes 284
  1.3 0.0 copy-start
  1.3 0.9 %copy-done = bf16[128,896]{1,0:T(8,128)(2,1)S(1)} copy-done((bf16[128,896]{1,0:T(8,128)(2,1)S(1)}, bf16[128,896]{1,0:T(8,128)(2,1)}, u32[]{:S(2)}) %copy-start) | copy-done | bytes 229400
  2.2 0.0 copy-start.1
  2.2 0.7 %copy-done.1 = bf16[128,64]{0,1:T(8,128)(2,1)S(1)} copy-done((bf16[128,64]{0,1:T(8,128)(2,1)S(1)}, bf16[128,64]{0,1:T(8,128)(2,1)}, u32[]{:S(2)}) %copy-start.1) | copy-done | bytes 16408
  2.9 34.1 %shard_map.50 = (bf16[3,128,128]{2,1,0:T(8,128)(2,1)S(1)}, f32[64,128]{1,0:T(8,128)S(1)}) custom-call(bf16[128,896]{1,0:T(8,128)(2,1)S(1)} %copy-done, f32[1,65]{1,0:T(1,128)S(1)} %bitcast.5, bf16[64,128]{1,0:T(8,128)(2,1)S(1)} %bitcast.4), custom_call_target="tpu_custom_call" | custom-call | tf_op jit(solution)/shard_map/pallas_call | solution.py:497
  37.1 0.6 %copy.7 = bf16[3,128,128]{2,1,0:T(8,128)(2,1)} copy(bf16[3,128,128]{2,1,0:T(8,128)(2,1)S(1)} %get-tuple-element.8) | data formatting | bytes 196608
  37.7 0.6 %copy.8 = f32[128,64]{0,1:T(8,128)} copy(f32[128,64]{0,1:T(8,128)S(1)} %bitcast.3) | data formatting | bytes 65536
Async XLA Ops:
  0.6 0.7 %copy-start.2 = (f32[65]{0:T(128)S(1)}, f32[65]{0:T(128)}, u32[]{:S(2)}) copy-start(f32[65]{0:T(128)} %param.4) | copy-start | bytes 784
  1.3 0.9 %copy-start = (bf16[128,896]{1,0:T(8,128)(2,1)S(1)}, bf16[128,896]{1,0:T(8,128)(2,1)}, u32[]{:S(2)}) copy-start(bf16[128,896]{1,0:T(8,128)(2,1)} %r_ref.1) | copy-start | bytes 688132
  2.2 0.7 %copy-start.1 = (bf16[128,64]{0,1:T(8,128)(2,1)S(1)}, bf16[128,64]{0,1:T(8,128)(2,1)}, u32[]{:S(2)}) copy-start(bf16[128,64]{0,1:T(8,128)(2,1)} %param.5) | copy-start | bytes 49156

commit v4 on v3

--- a/solution.py
+++ b/solution.py
@@ -368,6 +368,8 @@
         landed(z, other, c)
     block(z)
     take(1)
+    if chans > 2:
+        forward(2)
     for o in range(1, wins):
         image_landed(o).wait_recv()
     images = ib[0]
@@ -401,7 +403,9 @@
         take(h)
         return carry
 
-    lax.fori_loop(2, chans, hop, 0)
+    if chans > 2:
+        take(2)
+    lax.fori_loop(3, chans, hop, 0)
 
     def gram_landed(o, carry):
         gram_copy(o, True).wait_recv()

time: 38.6 us -> 37.2 us (0.964)
  the two profiles are of different devices: /device:TPU:29 before, /device:TPU:1 now
where the time goes in v4:
time: 37.2 us; the launch traced here: 36.9 us
  Pallas kernels  32.7 us (88%)
  local copies, waits for them, and re-layouts  3.56 us (10%)
  between operations  0.65 us (2%)
    pallas_call x1, Pallas kernels, body(): pl.pallas_call(functools.partial(kernel, chans, wins, width * wins), out_...  32.7 us
    unnamed x8, local copies, waits for them, and re-layouts  3.56 us

profile of v4, /device:TPU:1, one launch (start us, length us, event | category | flops | bytes accessed | tf_op | source)
XLA Modules:
  0.0 36.9 jit_solution(6991558658722048970)
XLA Ops:
  0.6 0.0 copy-start.2
  0.6 0.6 %copy-done.2 = f32[65]{0:T(128)S(1)} copy-done((f32[65]{0:T(128)S(1)}, f32[65]{0:T(128)}, u32[]{:S(2)}) %copy-start.2) | copy-done | bytes 284
  1.3 0.0 copy-start
  1.3 0.9 %copy-done = bf16[128,896]{1,0:T(8,128)(2,1)S(1)} copy-done((bf16[128,896]{1,0:T(8,128)(2,1)S(1)}, bf16[128,896]{1,0:T(8,128)(2,1)}, u32[]{:S(2)}) %copy-start) | copy-done | bytes 229400
  2.2 0.0 copy-start.1
  2.2 0.7 %copy-done.1 = bf16[128,64]{0,1:T(8,128)(2,1)S(1)} copy-done((bf16[128,64]{0,1:T(8,128)(2,1)S(1)}, bf16[128,64]{0,1:T(8,128)(2,1)}, u32[]{:S(2)}) %copy-start.1) | copy-done | bytes 16408
  2.9 32.7 %shard_map.50 = (bf16[3,128,128]{2,1,0:T(8,128)(2,1)S(1)}, f32[64,128]{1,0:T(8,128)S(1)}) custom-call(bf16[128,896]{1,0:T(8,128)(2,1)S(1)} %copy-done, f32[1,65]{1,0:T(1,128)S(1)} %bitcast.5, bf16[64,128]{1,0:T(8,128)(2,1)S(1)} %bitcast.4), custom_call_target="tpu_custom_call" | custom-call | tf_op jit(solution)/shard_map/pallas_call | solution.py:501
  35.7 0.6 %copy.7 = bf16[3,128,128]{2,1,0:T(8,128)(2,1)} copy(bf16[3,128,128]{2,1,0:T(8,128)(2,1)S(1)} %get-tuple-element.8) | data formatting | bytes 196608
  36.3 0.6 %copy.8 = f32[128,64]{0,1:T(8,128)} copy(f32[128,64]{0,1:T(8,128)S(1)} %bitcast.3) | data formatting | bytes 65536
Async XLA Ops:
  0.6 0.7 %copy-start.2 = (f32[65]{0:T(128)S(1)}, f32[65]{0:T(128)}, u32[]{:S(2)}) copy-start(f32[65]{0:T(128)} %param.4) | copy-start | bytes 784
  1.3 0.9 %copy-start = (bf16[128,896]{1,0:T(8,128)(2,1)S(1)}, bf16[128,896]{1,0:T(8,128)(2,1)}, u32[]{:S(2)}) copy-start(bf16[128,896]{1,0:T(8,128)(2,1)} %r_ref.1) | copy-start | bytes 688132
  2.2 0.7 %copy-start.1 = (bf16[128,64]{0,1:T(8,128)(2,1)S(1)}, bf16[128,64]{0,1:T(8,128)(2,1)}, u32[]{:S(2)}) copy-start(bf16[128,64]{0,1:T(8,128)(2,1)} %param.5) | copy-start | bytes 49156
